TPU v7x, 32 devices: a whole 2x2x4 slice. The times are simulated.
32 devices in a mesh: tm: 16 (over z, x, core), pairs: 2 (over y).
Axes of the slice: x: 2, y: 2, z: 4, core: 2. Of those that a mesh axis runs over, the one named last changes fastest.
Arguments:
- records: bfloat16 [2048, 65536], P('pairs', 'tm'), may hold values from -400 to 400
- station_order: int32 [2048], replicated, may hold values from 0 to 2047, each once
- block_list: int32 [20, 2], P('pairs'), may hold values from -1 to 31, as said below
Outputs:
- correlations: bfloat16 [20, 384, 2, 4096], P('pairs', 'tm')
Inputs may be any that keep to these rules, and one draw needn't show every extreme that they name: `station_order`: each station once. `block_list`: rows k * 10 to (k + 1) * 10 - 1 belong to owner k of the pairs axis; an owner's live blocks come first and its other rows hold -1 in both columns; some owner has all 10 rows live; in a live row the second group is the first plus 0 to 3, modulo 32.
All inputs are finite; a program needn't handle non-finite values.
Results may differ from a plain program's by a relative error of at most 0.0076.
Values may be sent and summed in bfloat16 or wider, within the bound.
A program may use at most 192 MiB of HBM per device.

v0:
```python
import math

import jax
import jax.numpy as jnp
from jax import lax
from jax.sharding import PartitionSpec as P

RECEIVER_TOTAL = 2048
GSIZE = 64
SUBWIN = 16
SAMPLES = 4096
TIME = 65536
BINS = 384
FIRST_BIN = 8
BAND = 64
HALF = 64


EPS = 1e-06


def dft_table():
    rows = jnp.arange(SAMPLES, dtype=jnp.int32)[:, None]
    cols = jnp.arange(BINS, dtype=jnp.int32)[None, :] + FIRST_BIN
    phase = (rows * cols % SAMPLES).astype(jnp.float32) * (2.0 * math.pi / SAMPLES)
    return jnp.concatenate([jnp.cos(phase), -jnp.sin(phase)], axis=1).astype(jnp.bfloat16)


def window_sum(values, width):
    length = values.shape[1]
    out_len = length - width + 1
    total = jnp.zeros((values.shape[0], out_len), jnp.float32)
    power = values
    size = 1
    offset = 0
    need = width
    while need > 0:
        if need % 2 == 1:
            total = total + power[:, offset : offset + out_len]
            offset = offset + size
        need = need // 2
        if need > 0:
            power = power[:, :-size] + power[:, size:]
            size = size * 2
    return total


def moving_norm(values, abs_padded, position):
    sums = window_sum(abs_padded, 2 * HALF + 1)
    upper = jnp.minimum(position + HALF, TIME - 1)
    lower = jnp.maximum(position - HALF, 0)
    counts = (upper - lower + 1).astype(jnp.float32)
    return (values.astype(jnp.float32) / (sums / counts + EPS)).astype(jnp.bfloat16)


def whiten(raw_rows):
    count = raw_rows.shape[0]
    parts = raw_rows.reshape(count, SUBWIN, 2, BINS // BAND, BAND)
    power = jnp.mean(parts[:, :, 0] ** 2 + parts[:, :, 1] ** 2, axis=-1)
    level = jnp.sqrt(power + EPS)
    return (parts / level[:, :, None, :, None]).reshape(count, SUBWIN, 2, BINS).astype(jnp.bfloat16)


def local(records, station_order, block_list):
    n_time = lax.axis_size("tm")
    n_owner = lax.axis_size("pairs")
    rows = lax.all_to_all(records, "tm", split_axis=0, concat_axis=1, tiled=True)
    magnitude = jnp.pad(jnp.abs(rows.astype(jnp.float32)), ((0, 0), (HALF, HALF)))
    normed = moving_norm(rows, magnitude, jnp.arange(TIME, dtype=jnp.int32))
    count = normed.shape[0]
    frames = normed.reshape(count * SUBWIN, SAMPLES)
    raw_rows = jnp.dot(frames, dft_table(), preferred_element_type=jnp.float32)
    whitened = whiten(raw_rows.reshape(count, SUBWIN, 2 * BINS))
    by_bin = jnp.transpose(whitened, (3, 1, 2, 0))
    collected = lax.all_gather(by_bin, "pairs", axis=3, tiled=True)
    mixed = lax.all_to_all(collected, "tm", split_axis=0, concat_axis=3, tiled=True)
    local_bins = mixed.shape[0]
    mixed = mixed.reshape(local_bins, SUBWIN, 2, n_time, n_owner, count)
    fourier_coefficients = jnp.transpose(mixed, (0, 1, 2, 4, 3, 5)).reshape(
        local_bins, SUBWIN, 2, RECEIVER_TOTAL
    )
    local_bins = fourier_coefficients.shape[0]
    slot_count = block_list.shape[0]
    group_members = station_order.reshape(-1, GSIZE)
    first = block_list[:, 0]
    second = block_list[:, 1]
    valid = (first >= 0).astype(jnp.float32)
    left_index = group_members[jnp.maximum(first, 0)].reshape(-1)
    right_index = group_members[jnp.maximum(second, 0)].reshape(-1)
    left = jnp.take(fourier_coefficients, left_index, axis=3).reshape(
        local_bins, SUBWIN * 2, slot_count, GSIZE
    )
    right = jnp.take(fourier_coefficients, right_index, axis=3).reshape(
        local_bins, SUBWIN, 2, slot_count, GSIZE
    )
    right_rows = right.reshape(local_bins, SUBWIN * 2, slot_count, GSIZE)
    turned = jnp.stack([right[:, :, 1], -right[:, :, 0]], axis=2).reshape(
        local_bins, SUBWIN * 2, slot_count, GSIZE
    )
    cosine_component = jnp.einsum(
        "fqki,fqkj->kfij", left, right_rows, preferred_element_type=jnp.float32
    )
    imag_part = jnp.einsum("fqki,fqkj->kfij", left, turned, preferred_element_type=jnp.float32)
    stacked = jnp.stack([cosine_component, imag_part], axis=2).reshape(
        slot_count, local_bins, 2, GSIZE * GSIZE
    )
    return (stacked * (valid / SUBWIN)[:, None, None, None]).astype(jnp.bfloat16)


def solution(mesh):
    placed = (P("pairs", "tm"), P(), P("pairs", None))
    return jax.shard_map(
        local, mesh=mesh, in_specs=placed, out_specs=P("pairs", "tm", None, None), check_vma=False
    )
```

profile of v0, /device:TPU:11, one launch (start us, length us, event | category | flops | bytes accessed | tf_op | source)
XLA Modules:
  0.0 684.6 jit_solution(2488591036763723454)
XLA Ops:
  6.5 6.6 all-to-all-start
  13.1 26.3 %cosine_convert_fusion = (bf16[4096,384]{0,1:T(8,128)(2,1)S(1)}, bf16[4096,384]{0,1:T(8,128)(2,1)S(1)}) fusion(s32[384]{0:T(512)S(1)} %iota_add_fusion.2), kind=kLoop, calls=%fused_computation.30 | loop fusion | flops 26738688 | bytes 6292992 | tf_op jit(solution)/shard_map/convert.2
  39.4 3.6 pad_maximum_fusion
  43.1 152.4 %all-to-all-done = bf16[16,64,4096]{2,1,0:T(8,128)(2,1)} async-done(((bf16[16,64,4096]{2,1,0:T(8,128)(2,1)}), bf16[16,64,4096]{2,1,0:T(8,128)(2,1)}, u32[]{:S(2)}, u32[]{:S(2)}) %all-to-all-start) | async-done | bytes 8388640 | tf_op jit(solution)/shard_map/all_to_all | solution.py:67
  195.4 11.4 %convert_bitcast_fusion = f32[16,8,8,4096]{3,2,1,0:T(8,128)} fusion(bf16[16,64,4096]{2,1,0:T(8,128)(2,1)} %all-to-all-done), kind=kLoop, calls=%fused_computation.15 | loop fusion | flops 4194304 | bytes 25165824
  206.8 6.6 copy.91
  213.4 5.7 copy-done
  219.2 6.1 abs.3
  225.3 17.2 %slice_add_fusion.5 = f32[64,65663]{1,0:T(8,128)S(1)} fusion(f32[64,65536]{1,0:T(8,128)} %abs.3), kind=kLoop, calls=%fused_computation.9 | loop fusion | flops 4202432 | bytes 33586944 | tf_op jit(solution)/shard_map/add | solution.py:43
  242.5 7.5 %slice_add_fusion.4 = f32[64,65661]{1,0:T(8,128)} fusion(f32[64,65663]{1,0:T(8,128)S(1)} %slice_add_fusion.5), kind=kLoop, calls=%fused_computation.8 | loop fusion | flops 4202304 | bytes 50427648 | tf_op jit(solution)/shard_map/add | solution.py:43
  250.0 14.7 %slice_add_fusion.3 = f32[64,65657]{1,0:T(8,128)S(1)} fusion(f32[64,65661]{1,0:T(8,128)} %slice_add_fusion.4), kind=kLoop, calls=%fused_computation.7 | loop fusion | flops 4202048 | bytes 50424576 | tf_op jit(solution)/shard_map/add | solution.py:43
  264.7 7.5 %slice_add_fusion.2 = f32[64,65649]{1,0:T(8,128)} fusion(f32[64,65657]{1,0:T(8,128)S(1)} %slice_add_fusion.3), kind=kLoop, calls=%fused_computation.6 | loop fusion | flops 4201536 | bytes 50418432 | tf_op jit(solution)/shard_map/add | solution.py:43
  272.3 19.2 %slice_add_fusion.1 = f32[64,65633]{1,0:T(8,128)} fusion(f32[64,65649]{1,0:T(8,128)} %slice_add_fusion.2), kind=kLoop, calls=%fused_computation.5 | loop fusion | flops 4200512 | bytes 50406144 | tf_op jit(solution)/shard_map/add | solution.py:43
  291.5 14.9 %slice_add_fusion = f32[64,65601]{1,0:T(8,128)S(1)} fusion(f32[64,65633]{1,0:T(8,128)} %slice_add_fusion.1), kind=kLoop, calls=%fused_computation.4 | loop fusion | flops 4198464 | bytes 50381568 | tf_op jit(solution)/shard_map/add | solution.py:43
  306.4 12.2 %fusion.27 = (f32[64,65537]{1,0:T(8,128)}, f32[64,65537]{1,0:T(8,128)}) fusion(f32[64,65601]{1,0:T(8,128)S(1)} %slice_add_fusion), kind=kLoop, calls=%fused_computation.67 | loop fusion | bytes 67109888 | tf_op jit(solution)/shard_map/slice | solution.py:43
  318.6 27.4 %fusion.4 = bf16[64,65536]{1,0:T(8,128)(2,1)} fusion(f32[64,65536]{1,0:T(8,128)} %bitcast.59, f32[64,65537]{1,0:T(8,128)} %get-tuple-element.7, f32[64,65537]{1,0:T(8,128)} %get-tuple-element.6, f32[64,65536]{1,0:T(8,128)} %abs.3, f32[65536]{0:T(1024)S(1)} %fusion.24), kind=kLoop, calls=%fused_computation.16 | loop fusion | flops 25165824 | bytes 75759616 | tf_op jit(solution)/shard_map/convert_element_type | solution.py:53
  346.0 12.0 %copy.92 = bf16[8,8,16,4096]{3,2,1,0:T(8,128)(2,1)} copy(bf16[8,8,16,4096]{3,1,2,0:T(8,128)(2,1)} %bitcast.60) | data formatting | bytes 16777216
  358.0 16.0 %fusion.5 = f32[64,16,2,6,64]{4,1,3,2,0:T(8,128)S(1)} fusion(bf16[2,6,64,4096,1]{3,2,1,0,4:T(8,128)(2,1)S(1)} %bitcast.70, bf16[64,16,4096,1,1]{2,1,0,3,4:T(8,128)(2,1)} %bitcast.66), kind=kOutput, calls=%fused_computation.20 | convolution fusion | flops 6442450944 | bytes 17825792 | tf_op jit(solution)/shard_map/dot_general | solution.py:72
  374.0 2.6 copy-done.1
  377.9 3.4 divide_convert_fusion
  381.3 3.9 copy.71
  385.2 6.1 convert_element_type.46
  391.3 44.6 %all-gather.2.cloned.1.call-done = bf16[384,16,2,128]{0,1,2,3:T(8,128)(2,1)} async-done(((bf16[384,16,2,64]{0,1,2,3:T(8,128)(2,1)}), bf16[384,16,2,128]{0,1,2,3:T(8,128)(2,1)}) %all-gather.2.cloned.1.call-update) | async-done | bytes 3145744 | tf_op jit(solution)/shard_map/all_gather | solution.py:75
  435.9 5.3 copy.72
  441.2 6.6 all-to-all-start.1
  449.3 68.3 %all-to-all-done.1 = bf16[384,16,2,128]{3,1,2,0:T(8,128)(2,1)S(1)} async-done(((bf16[384,16,2,128]{3,1,2,0:T(8,128)(2,1)}), bf16[384,16,2,128]{3,1,2,0:T(8,128)(2,1)S(1)}, u32[]{:S(2)}, u32[]{:S(2)}) %all-to-all-start.1) | async-done | bytes 3145760 | tf_op jit(solution)/shard_map/all_to_all | solution.py:76
  517.6 5.3 reshape.81
  523.0 28.2 %copy.88 = bf16[24,16,2,16,2,64]{0,1,5,3,4,2:T(8,128)(2,1)} copy(bf16[24,16,2,16,2,64]{5,4,1,2,0,3:T(2,128)(2,1)} %reshape.81) | data formatting | bytes 6291456 | tf_op jit(solution)/shard_map/transpose | solution.py:79
  551.2 10.4 %gather_fusion.3 = bf16[640,24,16,2]{1,2,3,0:T(8,128)(2,1)} fusion(bf16[24,16,2,2048]{0,1,3,2:T(8,128)(2,1)} %bitcast.62, s32[1024]{0:T(1024)S(1)} %pad_clamp_fusion), kind=kCustom, calls=%fused_computation.1.clone | custom fusion | bytes 1968640 | tf_op jit(solution)/shard_map/jit(_take)/gather | solution.py:93
  561.6 4.8 broadcast_select_fusion
  566.5 4.0 fusion.31
  570.4 2.9 fusion.28
  573.3 6.5 copy.90
  579.8 3.0 neg.8
  582.8 5.5 copy.89
  588.3 2.6 pad_maximum_fusion.1
  590.9 3.3 copy.81
  594.1 10.5 %gather_fusion.2 = bf16[640,24,16,2]{1,2,3,0:T(8,128)(2,1)} fusion(bf16[24,16,2,2048]{0,1,3,2:T(8,128)(2,1)} %bitcast.63, s32[1024]{0:T(1024)S(1)} %pad_clamp_fusion.2), kind=kCustom, calls=%fused_computation.clone | custom fusion | bytes 1968640 | tf_op jit(solution)/shard_map/jit(_take)/gather | solution.py:90
  604.6 7.0 %select_bitcast_fusion = bf16[24,16,2,640]{0,1,2,3:T(8,128)(2,1)} fusion(bf16[640,24,16,2]{1,2,3,0:T(8,128)(2,1)} %gather_fusion.2, pred[640]{0:T(1024)(128)(4,1)S(1)} %compare_and_fusion.1), kind=kLoop, calls=%fused_computation.34 | loop fusion | flops 491520 | bytes 1966720 | tf_op jit(solution)/shard_map/jit(_take)/select_n | solution.py:90
  611.6 5.8 copy.75
  617.4 3.3 reshape.85
  620.7 7.2 %fusion.18 = f32[10,24,64,64]{3,2,1,0:T(8,128)} fusion(bf16[24,32,10,64]{3,1,0,2:T(8,128)(2,1)} %bitcast.67, bf16[24,32,10,64]{3,2,0,1:T(8,128)(2,1)S(1)} %reshape.85), kind=kOutput, calls=%fused_computation.43 | convolution fusion | flops 62914560 | bytes 5898240 | tf_op jit(solution)/shard_map/fqki,fqkj->kfij/dot_general | solution.py:103
  627.8 8.8 %stack.18 = f32[10,24,1,4096]{3,2,1,0:T(1,128)} reshape(f32[10,24,64,64]{3,2,1,0:T(8,128)} %fusion.18) | data formatting | bytes 7864320 | tf_op jit(solution)/shard_map/stack | solution.py:104
  636.6 5.6 copy.77
  642.3 4.5 reshape_reshape.4
  646.8 10.3 %fusion.16 = f32[10,24,64,64]{3,2,1,0:T(8,128)} fusion(bf16[24,32,10,64]{3,2,0,1:T(8,128)(2,1)} %reshape_reshape.4, bf16[24,32,10,64]{3,2,0,1:T(8,128)(2,1)S(1)} %reshape.85), kind=kOutput, calls=%fused_computation.41 | convolution fusion | flops 62914560 | bytes 5898240 | tf_op jit(solution)/shard_map/fqki,fqkj->kfij/dot_general | solution.py:100
  657.1 9.1 %stack.17 = f32[10,24,1,4096]{3,2,1,0:T(1,128)} reshape(f32[10,24,64,64]{3,2,1,0:T(8,128)} %fusion.16) | data formatting | bytes 7864320 | tf_op jit(solution)/shard_map/stack | solution.py:104
  666.1 11.2 %fusion.7 = bf16[10,24,2,4096]{3,2,1,0:T(2,128)(2,1)} fusion(f32[10,24,1,4096]{3,2,1,0:T(1,128)} %stack.18, f32[10,24,1,4096]{3,2,1,0:T(1,128)} %stack.17, f32[10]{0:T(128)S(1)} %fusion.26), kind=kLoop, calls=%fused_computation.23 | loop fusion | flops 5898240 | bytes 11796520 | tf_op jit(solution)/shard_map/convert_element_type | solution.py:107
  (35 shorter events, 2.7 us)
Async XLA Ops:
  6.5 188.9 %all-to-all-start = ((bf16[16,64,4096]{2,1,0:T(8,128)(2,1)}), bf16[16,64,4096]{2,1,0:T(8,128)(2,1)}, u32[]{:S(2)}, u32[]{:S(2)}) async-start(bf16[16,64,4096]{2,1,0:T(8,128)(2,1)} %bitcast.65), calls=%async_computation | async-start | bytes 16777216 | tf_op jit(solution)/shard_map/all_to_all | solution.py:67
  13.1 422.8 %all-gather.2.cloned.1.call-start = ((), (), s32[]{:S(2)}) async-start(), calls=%async_computation.2 | async-start | bytes 4718592 | tf_op jit(solution)/shard_map/all_gather | solution.py:75
  213.4 5.7 copy-start
  306.4 51.7 %slice-start = ((s8[6291456]{0:T(1024)(128)(4,1)}), s8[2097152]{0:T(1024)(128)(4,1)S(1)}, s32[]{:S(2)}) async-start(s8[6291456]{0:T(1024)(128)(4,1)} %bitcast.68), calls=%async_computation.3 | async-start | bytes 4194304
  318.6 39.4 %slice-start.1 = ((s8[6291456]{0:T(1024)(128)(4,1)}), s8[4194304]{0:T(1024)(128)(4,1)S(1)}, s32[]{:S(2)}) async-start(s8[6291456]{0:T(1024)(128)(4,1)} %bitcast.68), calls=%async_computation.4 | async-start | bytes 8388608
  374.0 2.7 copy-start.1
  391.3 56.6 %copy-start.3 = (s32[2048]{0:T(1024)S(1)}, s32[2048]{0:T(1024)}, u32[]{:S(2)}) copy-start(s32[2048]{0:T(1024)} %param.6) | copy-start | bytes 24580
  391.3 56.6 %copy-start.4 = (s32[10,2]{0,1:T(2,128)S(1)}, s32[10,2]{0,1:T(2,128)}, u32[]{:S(2)}) copy-start(s32[10,2]{0,1:T(2,128)} %param.7) | copy-start | bytes 244
  441.2 76.4 %all-to-all-start.1 = ((bf16[384,16,2,128]{3,1,2,0:T(8,128)(2,1)}), bf16[384,16,2,128]{3,1,2,0:T(8,128)(2,1)S(1)}, u32[]{:S(2)}, u32[]{:S(2)}) async-start(bf16[384,16,2,128]{3,1,2,0:T(8,128)(2,1)} %copy.72), calls=%async_computation.1 | async-start | bytes 6291456 | tf_op jit(solution)/shard_map/all_to_all | solution.py:76
  561.6 4.8 copy-start.2
Sparse Core Ops, SparseCore 0:
  391.4 44.4 all-gather.1
where the time goes:
time: 695 us; the launch traced here: 685 us
  waiting for transfers between devices  265 us (38%)
  other arithmetic  193 us (28%)
  local copies, waits for them, and re-layouts  166 us (24%)
  matrix products  33.5 us (5%)
  between operations  14.1 us (2%)
  starting transfers between devices  13.2 us (2%)
    all_to_all x1, waiting for transfers between devices, local(): lax.all_to_all(records, 'tm', split_axis=0, concat_axis=1, tiled=True)  152 us
    add x6, other arithmetic, window_sum(): power = power[:, :-size] + power[:, size:]  81.1 us
    all_to_all x1, waiting for transfers between devices, local(): lax.all_to_all(collected, 'tm', split_axis=0, concat_axis=3, tiled=True)  68.3 us
    all_gather x1, waiting for transfers between devices, local(): collected = lax.all_gather(by_bin, 'pairs', axis=3, tiled=True)  44.6 us
    unnamed x17, local copies, waits for them, and re-layouts  32.3 us
    transpose x1, local copies, waits for them, and re-layouts, local(): jnp.transpose(mixed, (0, 1, 2, 4, 3, 5))  28.2 us
    convert_element_type x1, other arithmetic, moving_norm(): (values.astype(jnp.float32) / (sums / counts + EPS)).astype(jnp.bfloat16)  27.4 us
    another operation x1, other arithmetic  26.3 us
  transfers between devices with their start and end apart: 3, of which 3 were waited for; matrix products, arithmetic and copies ran while one was open for 5% of the time, Pallas kernels for 0%

commit v1 on v0

v1 whole, which is shorter than its diff:
```python
import functools
import math

import jax
import jax.numpy as jnp
import numpy as np
from jax import lax
from jax.experimental import pallas as pl
from jax.experimental.pallas import tpu as pltpu
from jax.sharding import PartitionSpec as P

GSIZE = 64
SUBWIN = 16
SAMPLES = 4096
TIME = 65536
BINS = 384
FIRST_BIN = 8
BAND = 64
HALF = 64
EPS = 1e-06

EDGE = 128
TILE = 256
MIB = 1 << 20
MESH = pl.DeviceIdType.MESH


def table_rows(bins_each):
    bins = np.arange(BINS, dtype=np.int64) + FIRST_BIN
    phase = np.outer(bins, np.arange(SAMPLES, dtype=np.int64)) % SAMPLES * (2.0 * math.pi / SAMPLES)
    both = np.stack([np.cos(phase), -np.sin(phase)])
    both = both.reshape(2, BINS // bins_each, bins_each, SAMPLES).transpose(1, 0, 2, 3)
    return both.reshape(2 * BINS, SAMPLES).astype(np.float32).astype(jnp.bfloat16)


def band_matrix():
    source = np.arange(TILE + 2 * EDGE)[:, None] - EDGE
    target = np.arange(TILE)[None, :]
    return (np.abs(source - target) <= HALF).astype(np.float32).astype(jnp.bfloat16)


def spectra_kernel(bins_each, x_ref, left_ref, right_ref, inv_ref, band_ref, table_ref, out_ref, mag_ref, norm_ref):
    rows = x_ref.shape[0]
    mag_ref[:, :EDGE] = jnp.abs(left_ref[...])
    mag_ref[:, EDGE : EDGE + SAMPLES] = jnp.abs(x_ref[...])
    mag_ref[:, EDGE + SAMPLES :] = jnp.abs(right_ref[...])
    for n in range(SAMPLES // TILE):
        cols = slice(n * TILE, (n + 1) * TILE)
        sums = jnp.dot(
            mag_ref[:, n * TILE : (n + 1) * TILE + 2 * EDGE], band_ref[...], preferred_element_type=jnp.float32
        )
        level = sums * inv_ref[:, cols] + EPS
        scaled = x_ref[:, cols].astype(jnp.float32) * pl.reciprocal(level, approx=True)
        norm_ref[:, cols] = scaled.astype(jnp.bfloat16)
    raw = lax.dot_general(
        table_ref[...], norm_ref[...], (((1,), (1,)), ((), ())), preferred_element_type=jnp.float32
    )
    parts = raw.reshape(BINS // bins_each, 2, bins_each, rows)
    power = (parts[:, 0] * parts[:, 0] + parts[:, 1] * parts[:, 1]).reshape(BINS // BAND, BAND, rows)
    scale = lax.rsqrt(jnp.sum(power, axis=1, keepdims=True) * (1.0 / BAND) + EPS)
    scale = jnp.broadcast_to(scale, (BINS // BAND, BAND, rows)).reshape(BINS // bins_each, 1, bins_each, rows)
    out_ref[...] = (parts * scale).reshape(BINS // bins_each, 2 * bins_each, rows).astype(jnp.bfloat16)


def spectra(x, left, right, inv, bins_each):
    count = x.shape[0]
    rows = min(256, count)
    whole = lambda i: (0, 0)
    by_row = lambda i: (i, 0)
    return pl.pallas_call(
        functools.partial(spectra_kernel, bins_each),
        grid=(count // rows,),
        in_specs=[
            pl.BlockSpec((rows, SAMPLES), by_row),
            pl.BlockSpec((rows, EDGE), by_row),
            pl.BlockSpec((rows, EDGE), by_row),
            pl.BlockSpec((1, SAMPLES), whole),
            pl.BlockSpec((TILE + 2 * EDGE, TILE), whole),
            pl.BlockSpec((2 * BINS, SAMPLES), whole),
        ],
        out_specs=pl.BlockSpec((BINS // bins_each, 2 * bins_each, rows), lambda i: (0, 0, i)),
        out_shape=jax.ShapeDtypeStruct((BINS // bins_each, 2 * bins_each, count), jnp.bfloat16),
        scratch_shapes=[
            pltpu.VMEM((rows, SAMPLES + 2 * EDGE), jnp.bfloat16),
            pltpu.VMEM((rows, SAMPLES), jnp.bfloat16),
        ],
        compiler_params=pltpu.CompilerParams(vmem_limit_bytes=48 * MIB),
    )(x, left, right, inv, jnp.asarray(band_matrix()), jnp.asarray(table_rows(bins_each)))


def exchange_kernel(n, s_ref, x_ref, own_sem, send_sem, recv_sem, hop_send, hop_recv):
    t = lax.axis_index("tm")
    p = lax.axis_index("pairs")
    other = 1 - p
    barrier = pltpu.get_barrier_semaphore()
    for d in range(1, n):
        pl.semaphore_signal(barrier, inc=1, device_id=(lax.rem(t + d, n), p), device_id_type=MESH)
    pl.semaphore_signal(barrier, inc=1, device_id=(t, other), device_id_type=MESH)
    pl.semaphore_wait(barrier, n)

    own = pltpu.make_async_copy(s_ref.at[t], x_ref.at[p, t], own_sem)
    own.start()
    copies = []
    for d in range(1, n):
        to = lax.rem(t + d, n)
        copies.append(
            pltpu.make_async_remote_copy(
                src_ref=s_ref.at[to],
                dst_ref=x_ref.at[p, t],
                send_sem=send_sem.at[d],
                recv_sem=recv_sem.at[d],
                device_id=(to, p),
                device_id_type=MESH,
            )
        )
        copies[-1].start()
    hops = []
    for d in range(n):
        source = lax.rem(t + n - d, n)
        if d:
            copies[d - 1].wait_recv()
        hops.append(
            pltpu.make_async_remote_copy(
                src_ref=x_ref.at[p, source] if d else s_ref.at[t],
                dst_ref=x_ref.at[p, source],
                send_sem=hop_send.at[d],
                recv_sem=hop_recv.at[d],
                device_id=(t, other),
                device_id_type=MESH,
            )
        )
        hops[-1].start()
    own.wait()
    for copy in copies:
        copy.wait_send()
    for hop in hops:
        hop.wait()


def exchange(mine):
    n, rows, count = mine.shape
    return pl.pallas_call(
        functools.partial(exchange_kernel, n),
        out_shape=jax.ShapeDtypeStruct((2, n, rows, count), jnp.bfloat16),
        in_specs=[pl.BlockSpec(memory_space=pl.ANY)],
        out_specs=pl.BlockSpec(memory_space=pl.ANY),
        scratch_shapes=[
            pltpu.SemaphoreType.DMA,
            pltpu.SemaphoreType.DMA((n,)),
            pltpu.SemaphoreType.DMA((n,)),
            pltpu.SemaphoreType.DMA((n,)),
            pltpu.SemaphoreType.DMA((n,)),
        ],
        compiler_params=pltpu.CompilerParams(collective_id=0, has_side_effects=True),
    )(mine)


def pairs_kernel(bins, step, blocks_ref, left_ids, right_ids, x_ref, out_ref, y_ref):
    halves, rows, count = x_ref.shape
    ids = []
    for s in range(step):
        k = pl.program_id(0) * step + s
        a = blocks_ref[k, 0]
        b = blocks_ref[k, 1]
        live = a >= 0
        ids.append(jnp.where(live, left_ids[pl.ds(jnp.maximum(a, 0), 1), :], -1))
        ids.append(jnp.where(live, right_ids[pl.ds(jnp.maximum(b, 0), 1), :], -1))
    wanted = jnp.concatenate(ids, axis=1)
    station = lax.broadcasted_iota(jnp.int32, (count, step * 256), 0)
    total = None
    for h in range(halves):
        pick = jnp.where(station == wanted - h * count, 1.0, 0.0).astype(jnp.bfloat16)
        part = jnp.dot(x_ref[h], pick, preferred_element_type=jnp.float32)
        total = part if total is None else total + part
    for n in range(2 * step):
        y_ref[n] = total[:, n * 128 : (n + 1) * 128]
    lane = lax.broadcasted_iota(jnp.int32, (SUBWIN, 128), 1)
    straight = lane % 2 == 0
    low = lax.broadcasted_iota(jnp.int32, (GSIZE, 128), 1) < GSIZE
    for f in range(bins):
        for s in range(step):
            re_a = y_ref[2 * s, pl.ds(f, SUBWIN, stride=2 * bins), :]
            im_a = y_ref[2 * s, pl.ds(bins + f, SUBWIN, stride=2 * bins), :]
            re_b = y_ref[2 * s + 1, pl.ds(f, SUBWIN, stride=2 * bins), :]
            im_b = y_ref[2 * s + 1, pl.ds(bins + f, SUBWIN, stride=2 * bins), :]
            a_rows = jnp.concatenate(
                [jnp.where(straight, re_a, -im_a), jnp.where(straight, im_a, re_a)], axis=0
            ).astype(jnp.bfloat16)
            b_rows = jnp.concatenate([re_b, im_b], axis=0).astype(jnp.bfloat16)
            full = lax.dot_general(
                a_rows, b_rows, (((0,), (0,)), ((), ())), preferred_element_type=jnp.float32
            )
            kept = jnp.where(low, full[:GSIZE], full[GSIZE:]) * (1.0 / SUBWIN)
            out_ref[s, f] = kept.astype(jnp.bfloat16)


def correlate(x, station_order, block_list, bins):
    slots = block_list.shape[0]
    halves, rows, count = x.shape
    groups = station_order.reshape(-1, GSIZE)
    n_groups = groups.shape[0]
    left_ids = groups.reshape(n_groups, GSIZE // 2, 2).transpose(0, 2, 1)
    left_ids = jnp.repeat(left_ids.reshape(n_groups, GSIZE), 2, axis=1)
    right_ids = jnp.concatenate([groups, groups], axis=1)
    step = 2 if slots % 2 == 0 else 1
    out = pl.pallas_call(
        functools.partial(pairs_kernel, bins, step),
        grid_spec=pltpu.PrefetchScalarGridSpec(
            num_scalar_prefetch=1,
            grid=(slots // step,),
            in_specs=[
                pl.BlockSpec((n_groups, 128), lambda i, b: (0, 0)),
                pl.BlockSpec((n_groups, 128), lambda i, b: (0, 0)),
                pl.BlockSpec((halves, rows, count), lambda i, b: (0, 0, 0)),
            ],
            out_specs=pl.BlockSpec((step, bins, GSIZE, 128), lambda i, b: (i, 0, 0, 0)),
            scratch_shapes=[pltpu.VMEM((2 * step, rows, 128), jnp.float32)],
        ),
        out_shape=jax.ShapeDtypeStruct((slots, bins, GSIZE, 128), jnp.bfloat16),
        compiler_params=pltpu.CompilerParams(vmem_limit_bytes=48 * MIB),
    )(block_list, left_ids, right_ids, x)
    out = out.reshape(slots, bins, GSIZE // 2, 2, 128).transpose(0, 1, 3, 2, 4)
    return out.reshape(slots, bins, 2, GSIZE * GSIZE)


def local(records, station_order, block_list):
    n = lax.axis_size("tm")
    owners = lax.axis_size("pairs")
    share = SAMPLES // records.shape[1]
    x = records
    if share > 1:
        sets = [list(range(i, i + share)) for i in range(0, n, share)]
        x = lax.all_to_all(x, "tm", split_axis=0, concat_axis=1, axis_index_groups=sets, tiled=True)
    count = x.shape[0]
    left = lax.ppermute(x[:, -EDGE:], "tm", [(i, i + share) for i in range(n - share)])
    right = lax.ppermute(x[:, :EDGE], "tm", [(i + share, i) for i in range(n - share)])
    position = lax.axis_index("tm") // share * SAMPLES + jnp.arange(SAMPLES, dtype=jnp.int32)
    upper = jnp.minimum(position + HALF, TIME - 1)
    lower = jnp.maximum(position - HALF, 0)
    inv = (1.0 / (upper - lower + 1).astype(jnp.float32))[None, :]
    bins = BINS // n
    rows = SUBWIN * 2 * bins
    if share == 1 and owners == 2 and bins % 8 == 0:
        gathered = exchange(spectra(x, left, right, inv, bins)).reshape(owners, rows, count)
    else:
        mine = spectra(x, left, right, inv, BINS).reshape(2, n, bins, count)
        mine = lax.all_to_all(mine.transpose(1, 0, 2, 3), "tm", split_axis=0, concat_axis=0, tiled=True)
        mine = mine.reshape(SUBWIN, share, 2, bins, count).transpose(0, 2, 3, 1, 4)
        gathered = lax.all_gather(mine.reshape(rows, share * count), "pairs", axis=0)
    return correlate(gathered, station_order, block_list, bins)


def solution(mesh):
    placed = (P("pairs", "tm"), P(), P("pairs", None))
    return jax.shard_map(
        local, mesh=mesh, in_specs=placed, out_specs=P("pairs", "tm", None, None), check_vma=False
    )
```

time: 695 us -> 105 us (0.15)
  the two profiles are of different devices: /device:TPU:11 before, /device:TPU:25 now
where the time goes in v1:
time: 105 us; the launch traced here: 104 us
  Pallas kernels  90.3 us (86%)
  local copies, waits for them, and re-layouts  8.18 us (8%)
  starting transfers between devices  5.6 us (5%)
    pallas_call x1, Pallas kernels, exchange(): pl.pallas_call(functools.partial(exchange_kernel, n), out_shape=jax.Shape...  60.6 us
    pallas_call x1, Pallas kernels, spectra(): pl.pallas_call(functools.partial(spectra_kernel, bins_each), grid=(count...  15.5 us
    pallas_call x1, Pallas kernels, correlate(): pl.pallas_call(functools.partial(pairs_kernel, bins, step), grid_spec=plt...  14.1 us
    unnamed x7, local copies, waits for them, and re-layouts  4.74 us
    ppermute x1, starting transfers between devices, local(): lax.ppermute(x[:, -EDGE:], 'tm', [(i, i + share) for i in range(n - share)])  3.02 us
    ppermute x1, starting transfers between devices, local(): lax.ppermute(x[:, :EDGE], 'tm', [(i + share, i) for i in range(n - share)])  2.58 us
  transfers between devices with their start and end apart: 2, of which 0 were waited for; matrix products, arithmetic and copies ran while one was open for 3% of the time, Pallas kernels for 0%

profile of v1, /device:TPU:25, one launch (start us, length us, event | category | flops | bytes accessed | tf_op | source)
XLA Modules:
  0.0 104.3 jit_solution(10248375789420033536)
XLA Ops:
  0.0 1.1 %fusion = (bf16[1024,128]{1,0:T(8,128)(2,1)S(1)}, bf16[1024,128]{1,0:T(8,128)(2,1)S(1)}) fusion(bf16[1024,4096]{1,0:T(8,128)(2,1)} %x_ref.1), kind=kLoop, calls=%fused_computation.2 | loop fusion | bytes 1048576 | tf_op jit(solution)/shard_map/slice | solution.py:236
  1.1 2.6 %collective-permute-start.1 = (bf16[1024,128]{1,0:T(8,128)(2,1)S(1)}, bf16[1024,128]{1,0:T(8,128)(2,1)S(1)}, u32[]{:S(2)}, u32[]{:S(2)}) collective-permute-start(bf16[1024,128]{1,0:T(8,128)(2,1)S(1)} %get-tuple-element.5), channel_id=1, source_target_pairs={{2,0},{4,2},{6,4},{8,6},{10,8},{12,10},{14,12},{16,14},{18,16},{20... | collective-permute-start | bytes 786440 | tf_op jit(solution)/shard_map/ppermute | solution.py:236
  3.7 3.0 %collective-permute-start = (bf16[1024,128]{1,0:T(8,128)(2,1)S(1)}, bf16[1024,128]{1,0:T(8,128)(2,1)S(1)}, u32[]{:S(2)}, u32[]{:S(2)}) collective-permute-start(bf16[1024,128]{1,0:T(8,128)(2,1)S(1)} %get-tuple-element.6), channel_id=1, source_target_pairs={{0,2},{2,4},{4,6},{6,8},{8,10},{10,12},{12,14},{14,16},{16,18},{18... | collective-permute-start | bytes 786440 | tf_op jit(solution)/shard_map/ppermute | solution.py:235
  6.7 0.1 convert_divide_fusion.inv_ref
  6.8 0.8 reshape.51
  7.5 1.2 %reshape_reshape.3 = s32[32,32,2]{2,1,0:T(8,128)S(1)} reshape(s32[2048]{0:T(1024)} %param.6) | data formatting | bytes 16384 | tf_op jit(solution)/shard_map/reshape;reshape | solution.py:202
  8.7 0.8 copy.13.blocks_ref
  9.5 0.4 copy.16
  9.9 0.1 copy.14.left_ids
  9.9 0.1 pad_add_fusion.right_ids
  10.0 0.0 collective-permute-done.1.right_ref
  10.0 0.0 collective-permute-done.left_ref
  10.0 0.0 copy-start.2
  10.0 0.9 copy-done.2
  11.0 15.5 %shard_map.55.s_ref = bf16[16,48,1024]{2,1,0:T(8,128)(2,1)S(1)} custom-call(bf16[1024,4096]{1,0:T(8,128)(2,1)} %x_ref.1, bf16[1024,128]{1,0:T(8,128)(2,1)S(1)} %collective-permute-done.left_ref, bf16[1024,128]{1,0:T(8,128)(2,1)S(1)} %collective-permute-done.1.right_ref, f32[1,4096]{1,0:T(1,128)S(1)} %convert_divide_fusion.inv_ref, ...), custom_call_target="tpu_custom_call" | custom-call | tf_op jit(solution)/shard_map/pallas_call | solution.py:70
  26.5 0.0 copy-start.1
  26.5 1.1 %copy-done.1 = bf16[16,48,1024]{2,1,0:T(8,128)(2,1)} copy-done((bf16[16,48,1024]{2,1,0:T(8,128)(2,1)}, bf16[16,48,1024]{2,1,0:T(8,128)(2,1)S(1)}, u32[]{:S(2)}) %copy-start.1) | copy-done | bytes 1572888
  27.7 60.6 %shard_map.56 = bf16[2,16,48,1024]{3,2,1,0:T(8,128)(2,1)} custom-call(bf16[16,48,1024]{2,1,0:T(8,128)(2,1)} %copy-done.1), custom_call_target="tpu_custom_call" | custom-call | tf_op jit(solution)/shard_map/pallas_call | solution.py:142
  88.3 0.0 copy-start
  88.3 1.9 %copy-done = bf16[2,16,48,1024]{3,2,1,0:T(8,128)(2,1)S(1)} copy-done((bf16[2,16,48,1024]{3,2,1,0:T(8,128)(2,1)S(1)}, bf16[2,16,48,1024]{3,2,1,0:T(8,128)(2,1)}, u32[]{:S(2)}) %copy-start) | copy-done | bytes 3145752
  90.2 14.1 %shard_map.57 = bf16[10,24,64,128]{3,2,1,0:T(8,128)(2,1)} custom-call(s32[10,2]{1,0:T(8,128)S(1)} %copy.13.blocks_ref, s32[32,128]{1,0:T(8,128)S(1)} %copy.14.left_ids, s32[32,128]{1,0:T(8,128)S(1)} %pad_add_fusion.right_ids, bf16[2,768,1024]{2,1,0:T(8,128)(2,1)S(1)} %bitcast.9), custom_call_target="tpu_custom_call" | custom-call | tf_op jit(solution)/shard_map/pallas_call | solution.py:206
  (1 shorter events, 0.0 us)
Async XLA Ops:
  1.1 8.9 %collective-permute-start.1 = (bf16[1024,128]{1,0:T(8,128)(2,1)S(1)}, bf16[1024,128]{1,0:T(8,128)(2,1)S(1)}, u32[]{:S(2)}, u32[]{:S(2)}) collective-permute-start(bf16[1024,128]{1,0:T(8,128)(2,1)S(1)} %get-tuple-element.5), channel_id=1, source_target_pairs={{2,0},{4,2},{6,4},{8,6},{10,8},{12,10},{14,12},{16,14},{18,16},{20... | collective-permute-start | bytes 786440 | tf_op jit(solution)/shard_map/ppermute | solution.py:236
  3.7 6.3 %collective-permute-start = (bf16[1024,128]{1,0:T(8,128)(2,1)S(1)}, bf16[1024,128]{1,0:T(8,128)(2,1)S(1)}, u32[]{:S(2)}, u32[]{:S(2)}) collective-permute-start(bf16[1024,128]{1,0:T(8,128)(2,1)S(1)} %get-tuple-element.6), channel_id=1, source_target_pairs={{0,2},{2,4},{4,6},{6,8},{8,10},{10,12},{12,14},{14,16},{16,18},{18... | collective-permute-start | bytes 786440 | tf_op jit(solution)/shard_map/ppermute | solution.py:235
  10.0 1.0 copy-start.2
  26.5 1.1 %copy-start.1 = (bf16[16,48,1024]{2,1,0:T(8,128)(2,1)}, bf16[16,48,1024]{2,1,0:T(8,128)(2,1)S(1)}, u32[]{:S(2)}) copy-start(bf16[16,48,1024]{2,1,0:T(8,128)(2,1)S(1)} %shard_map.55.s_ref) | copy-start | bytes 4718596
  88.3 1.9 %copy-start = (bf16[2,16,48,1024]{3,2,1,0:T(8,128)(2,1)S(1)}, bf16[2,16,48,1024]{3,2,1,0:T(8,128)(2,1)}, u32[]{:S(2)}) copy-start(bf16[2,16,48,1024]{3,2,1,0:T(8,128)(2,1)} %shard_map.56) | copy-start | bytes 9437188

commit v2 on v1

v2 whole, which is shorter than its diff:
```python
import functools
import math

import jax
import jax.numpy as jnp
import numpy as np
from jax import lax
from jax.experimental import pallas as pl
from jax.experimental.pallas import tpu as pltpu
from jax.sharding import PartitionSpec as P

GSIZE = 64
SUBWIN = 16
SAMPLES = 4096
TIME = 65536
BINS = 384
FIRST_BIN = 8
BAND = 64
HALF = 64
EPS = 1e-06

EDGE = 128
TILE = 256
MIB = 1 << 20
MESH = pl.DeviceIdType.MESH


def table_rows(bins_each):
    bins = np.arange(BINS, dtype=np.int64) + FIRST_BIN
    phase = np.outer(bins, np.arange(SAMPLES, dtype=np.int64)) % SAMPLES * (2.0 * math.pi / SAMPLES)
    both = np.stack([np.cos(phase), -np.sin(phase)])
    both = both.reshape(2, BINS // bins_each, bins_each, SAMPLES).transpose(1, 0, 2, 3)
    return both.reshape(2 * BINS, SAMPLES).astype(np.float32).astype(jnp.bfloat16)


def normalise(x_ref, norm_ref, mag_ref, band_ref, start):
    for n in range(SAMPLES // TILE):
        cols = slice(n * TILE, (n + 1) * TILE)
        sums = jnp.dot(
            mag_ref[:, n * TILE : (n + 1) * TILE + 2 * EDGE], band_ref[...], preferred_element_type=jnp.float32
        )
        position = start + n * TILE + lax.broadcasted_iota(jnp.int32, (1, TILE), 1)
        upper = jnp.minimum(position + HALF, TIME - 1)
        lower = jnp.maximum(position - HALF, 0)
        inv = 1.0 / (upper - lower + 1).astype(jnp.float32)
        scaled = x_ref[:, cols].astype(jnp.float32) * pl.reciprocal(sums * inv + EPS, approx=True)
        norm_ref[:, cols] = scaled.astype(jnp.bfloat16)


def fill_band(band_ref):
    source = lax.broadcasted_iota(jnp.int32, band_ref.shape, 0) - EDGE
    target = lax.broadcasted_iota(jnp.int32, band_ref.shape, 1)
    band_ref[...] = jnp.where(jnp.abs(source - target) <= HALF, 1.0, 0.0).astype(jnp.bfloat16)


def transform(table_ref, norm_ref, bins_each):
    rows = norm_ref.shape[0]
    raw = lax.dot_general(
        table_ref[...], norm_ref[...], (((1,), (1,)), ((), ())), preferred_element_type=jnp.float32
    )
    parts = raw.reshape(BINS // bins_each, 2, bins_each, rows)
    power = (parts[:, 0] * parts[:, 0] + parts[:, 1] * parts[:, 1]).reshape(BINS // BAND, BAND, rows)
    scale = lax.rsqrt(jnp.sum(power, axis=1, keepdims=True) * (1.0 / BAND) + EPS)
    scale = jnp.broadcast_to(scale, (BINS // BAND, BAND, rows)).reshape(BINS // bins_each, 1, bins_each, rows)
    return (parts * scale).reshape(BINS // bins_each, 2 * bins_each, rows).astype(jnp.bfloat16)


def spectra_kernel(share, x_ref, left_ref, right_ref, table_ref, out_ref, mag_ref, norm_ref, band_ref):
    @pl.when(pl.program_id(0) == 0)
    def _():
        fill_band(band_ref)

    mag_ref[:, :EDGE] = jnp.abs(left_ref[...])
    mag_ref[:, EDGE : EDGE + SAMPLES] = jnp.abs(x_ref[...])
    mag_ref[:, EDGE + SAMPLES :] = jnp.abs(right_ref[...])
    normalise(x_ref, norm_ref, mag_ref, band_ref, lax.div(lax.axis_index("tm"), share) * SAMPLES)
    out_ref[...] = transform(table_ref, norm_ref, BINS)


def spectra(x, left, right, share):
    count = x.shape[0]
    rows = min(256, count)
    whole = lambda i: (0, 0)
    by_row = lambda i: (i, 0)
    return pl.pallas_call(
        functools.partial(spectra_kernel, share),
        grid=(count // rows,),
        in_specs=[
            pl.BlockSpec((rows, SAMPLES), by_row),
            pl.BlockSpec((rows, EDGE), by_row),
            pl.BlockSpec((rows, EDGE), by_row),
            pl.BlockSpec((2 * BINS, SAMPLES), whole),
        ],
        out_specs=pl.BlockSpec((1, 2 * BINS, rows), lambda i: (0, 0, i)),
        out_shape=jax.ShapeDtypeStruct((1, 2 * BINS, count), jnp.bfloat16),
        scratch_shapes=[
            pltpu.VMEM((rows, SAMPLES + 2 * EDGE), jnp.bfloat16),
            pltpu.VMEM((rows, SAMPLES), jnp.bfloat16),
            pltpu.VMEM((TILE + 2 * EDGE, TILE), jnp.bfloat16),
        ],
        compiler_params=pltpu.CompilerParams(vmem_limit_bytes=48 * MIB),
    )(x, left, right, jnp.asarray(table_rows(BINS)))


def fused_kernel(n, bins, blocks, rec_ref, x_ref, table_hbm, got_ref, mag_ref, norm_ref, band_ref, table_ref,
                 left_ref, right_ref, mine_ref, table_sem, edge_send, edge_recv, own_sem, send_sem, recv_sem,
                 hop_send, hop_recv):
    t = lax.axis_index("tm")
    p = lax.axis_index("pairs")
    i = pl.program_id(0)
    rows = x_ref.shape[0]
    count = rows * blocks
    other = 1 - p
    after, before = lax.rem(t + 1, n), lax.rem(t + n - 1, n)
    table_copy = pltpu.make_async_copy(table_hbm, table_ref, table_sem)

    def columns(block):
        return pl.ds(pl.multiple_of(p * count + block * rows, 128), rows)

    def direct(block, d):
        to = lax.rem(t + d, n)
        return pltpu.make_async_remote_copy(
            src_ref=mine_ref.at[block, to],
            dst_ref=got_ref.at[t, :, columns(block)],
            send_sem=send_sem.at[block, d],
            recv_sem=recv_sem.at[block, d],
            device_id=(to, p),
            device_id_type=MESH,
        )

    def hop(block, d):
        source = lax.rem(t + n - d, n)
        return pltpu.make_async_remote_copy(
            src_ref=got_ref.at[source, :, columns(block)] if d else mine_ref.at[block, t],
            dst_ref=got_ref.at[source, :, columns(block)],
            send_sem=hop_send.at[block, d],
            recv_sem=hop_recv.at[block, d],
            device_id=(t, other),
            device_id_type=MESH,
        )

    def own(block):
        return pltpu.make_async_copy(mine_ref.at[block, t], got_ref.at[t, :, columns(block)], own_sem.at[block])

    def forward(block):
        for d in range(1, n):
            direct(block, d).wait_recv()
            hop(block, d).start()

    @pl.when(i == 0)
    def _():
        table_copy.start()
        barrier = pltpu.get_barrier_semaphore()
        for d in range(1, n):
            pl.semaphore_signal(barrier, inc=1, device_id=(lax.rem(t + d, n), p), device_id_type=MESH)
        pl.semaphore_signal(barrier, inc=1, device_id=(t, other), device_id_type=MESH)
        fill_band(band_ref)
        pl.semaphore_wait(barrier, n)
        edges = [
            pltpu.make_async_remote_copy(
                src_ref=rec_ref.at[:, pl.ds(first, EDGE)],
                dst_ref=landing,
                send_sem=edge_send.at[k],
                recv_sem=edge_recv.at[k],
                device_id=(to, p),
                device_id_type=MESH,
            )
            for k, (first, landing, to) in enumerate(
                [(SAMPLES - EDGE, left_ref, after), (0, right_ref, before)]
            )
        ]
        for edge in edges:
            edge.start()
        for edge in edges:
            edge.wait()

    at = pl.ds(pl.multiple_of(i * rows, rows), rows)
    left = jnp.abs(left_ref[at, :])
    right = jnp.abs(right_ref[at, :])
    mag_ref[:, :EDGE] = jnp.where(t == 0, jnp.zeros_like(left), left)
    mag_ref[:, EDGE : EDGE + SAMPLES] = jnp.abs(x_ref[...])
    mag_ref[:, EDGE + SAMPLES :] = jnp.where(t == n - 1, jnp.zeros_like(right), right)
    normalise(x_ref, norm_ref, mag_ref, band_ref, t * SAMPLES)

    @pl.when(i == 0)
    def _():
        table_copy.wait()

    mine_ref[i] = transform(table_ref, norm_ref, bins)
    for d in range(1, n):
        direct(i, d).start()
    hop(i, 0).start()
    own(i).start()

    @pl.when(i > 0)
    def _():
        forward(i - 1)

    @pl.when(i == blocks - 1)
    def _():
        forward(blocks - 1)

        def finish(block, carry):
            own(block).wait()
            for d in range(n):
                if d:
                    direct(block, d).wait_send()
                hop(block, d).wait()
            return carry

        lax.fori_loop(0, blocks, finish, 0)


def fused(records, n, bins):
    count = records.shape[0]
    rows = 256
    blocks = count // rows
    chunk = 2 * bins
    return pl.pallas_call(
        functools.partial(fused_kernel, n, bins, blocks),
        grid=(blocks,),
        in_specs=[
            pl.BlockSpec(memory_space=pl.ANY),
            pl.BlockSpec((rows, SAMPLES), lambda i: (i, 0)),
            pl.BlockSpec(memory_space=pl.ANY),
        ],
        out_specs=pl.BlockSpec(memory_space=pl.ANY),
        out_shape=jax.ShapeDtypeStruct((n, chunk, 2 * count), jnp.bfloat16),
        scratch_shapes=[
            pltpu.VMEM((rows, SAMPLES + 2 * EDGE), jnp.bfloat16),
            pltpu.VMEM((rows, SAMPLES), jnp.bfloat16),
            pltpu.VMEM((TILE + 2 * EDGE, TILE), jnp.bfloat16),
            pltpu.VMEM((2 * BINS, SAMPLES), jnp.bfloat16),
            pltpu.VMEM((count, EDGE), jnp.bfloat16),
            pltpu.VMEM((count, EDGE), jnp.bfloat16),
            pltpu.VMEM((blocks, n, chunk, rows), jnp.bfloat16),
            pltpu.SemaphoreType.DMA,
            pltpu.SemaphoreType.DMA((2,)),
            pltpu.SemaphoreType.DMA((2,)),
            pltpu.SemaphoreType.DMA((blocks,)),
            pltpu.SemaphoreType.DMA((blocks, n)),
            pltpu.SemaphoreType.DMA((blocks, n)),
            pltpu.SemaphoreType.DMA((blocks, n)),
            pltpu.SemaphoreType.DMA((blocks, n)),
        ],
        compiler_params=pltpu.CompilerParams(
            collective_id=0, has_side_effects=True, vmem_limit_bytes=48 * MIB
        ),
    )(records, records, jnp.asarray(table_rows(bins)))


def slot_ids(order_ref, group, live, lanes):
    group = jnp.maximum(group, 0)
    row = order_ref[pl.ds(group // 2, 1), :]
    high, low = lax.shift_right_logical(row, 5), lax.bitwise_and(row, 31)
    digits = jnp.where(lax.broadcasted_iota(jnp.int32, (16, 128), 0) == 0, high, low)
    member = lanes + (group % 2) * GSIZE
    pick = jnp.where(lax.broadcasted_iota(jnp.int32, (128, 128), 0) == member, 1.0, 0.0)
    moved = jnp.dot(
        digits.astype(jnp.float32).astype(jnp.bfloat16),
        pick.astype(jnp.bfloat16),
        preferred_element_type=jnp.float32,
    )
    ids = (moved[0:1] * 32.0 + moved[1:2]).astype(jnp.int32)
    return jnp.where(live, ids, -1)


def pairs_kernel(bins, step, blocks_ref, order_ref, x_ref, out_ref, y_ref):
    ids = []
    lane = lax.broadcasted_iota(jnp.int32, (1, 128), 1)
    left_lanes = lane % GSIZE // 2 * 2 + lane // GSIZE
    right_lanes = lane % GSIZE
    for s in range(step):
        k = pl.program_id(0) * step + s
        live = blocks_ref[k, 0] >= 0
        ids.append(slot_ids(order_ref, blocks_ref[k, 0], live, left_lanes))
        ids.append(slot_ids(order_ref, blocks_ref[k, 1], live, right_lanes))
    wanted = jnp.concatenate(ids, axis=1)
    station = lax.broadcasted_iota(jnp.int32, (x_ref.shape[1], step * 256), 0)
    pick = jnp.where(station == wanted, 1.0, 0.0).astype(jnp.bfloat16)
    total = jnp.dot(x_ref[...], pick, preferred_element_type=jnp.float32)
    for n in range(2 * step):
        y_ref[n] = total[:, n * 128 : (n + 1) * 128]
    lane = lax.broadcasted_iota(jnp.int32, (SUBWIN, 128), 1)
    straight = lane % 2 == 0
    low = lax.broadcasted_iota(jnp.int32, (GSIZE, 128), 1) < GSIZE
    for f in range(bins):
        for s in range(step):
            re_a = y_ref[2 * s, pl.ds(f, SUBWIN, stride=2 * bins), :]
            im_a = y_ref[2 * s, pl.ds(bins + f, SUBWIN, stride=2 * bins), :]
            re_b = y_ref[2 * s + 1, pl.ds(f, SUBWIN, stride=2 * bins), :]
            im_b = y_ref[2 * s + 1, pl.ds(bins + f, SUBWIN, stride=2 * bins), :]
            a_rows = jnp.concatenate(
                [jnp.where(straight, re_a, -im_a), jnp.where(straight, im_a, re_a)], axis=0
            ).astype(jnp.bfloat16)
            b_rows = jnp.concatenate([re_b, im_b], axis=0).astype(jnp.bfloat16)
            full = lax.dot_general(
                a_rows, b_rows, (((0,), (0,)), ((), ())), preferred_element_type=jnp.float32
            )
            kept = jnp.where(low, full[:GSIZE], full[GSIZE:]) * (1.0 / SUBWIN)
            out_ref[s, f] = kept.astype(jnp.bfloat16)


def correlate(x, station_order, block_list, bins):
    slots = block_list.shape[0]
    rows, stations = x.shape
    order = station_order.reshape(-1, 128)
    step = 2 if slots % 2 == 0 else 1
    out = pl.pallas_call(
        functools.partial(pairs_kernel, bins, step),
        grid_spec=pltpu.PrefetchScalarGridSpec(
            num_scalar_prefetch=1,
            grid=(slots // step,),
            in_specs=[
                pl.BlockSpec(order.shape, lambda i, b: (0, 0)),
                pl.BlockSpec((rows, stations), lambda i, b: (0, 0)),
            ],
            out_specs=pl.BlockSpec((step, bins, GSIZE, 128), lambda i, b: (i, 0, 0, 0)),
            scratch_shapes=[pltpu.VMEM((2 * step, rows, 128), jnp.float32)],
        ),
        out_shape=jax.ShapeDtypeStruct((slots, bins, GSIZE, 128), jnp.bfloat16),
        compiler_params=pltpu.CompilerParams(vmem_limit_bytes=48 * MIB),
    )(block_list, order, x)
    out = out.reshape(slots, bins, GSIZE // 2, 2, 128).transpose(0, 1, 3, 2, 4)
    return out.reshape(slots, bins, 2, GSIZE * GSIZE)


def local(records, station_order, block_list):
    n = lax.axis_size("tm")
    owners = lax.axis_size("pairs")
    share = SAMPLES // records.shape[1]
    bins = BINS // n
    rows = SUBWIN * 2 * bins
    if share == 1 and owners == 2 and bins % 8 == 0:
        return correlate(fused(records, n, bins).reshape(rows, -1), station_order, block_list, bins)
    x = records
    if share > 1:
        sets = [list(range(i, i + share)) for i in range(0, n, share)]
        x = lax.all_to_all(x, "tm", split_axis=0, concat_axis=1, axis_index_groups=sets, tiled=True)
    count = x.shape[0]
    left = lax.ppermute(x[:, -EDGE:], "tm", [(i, i + share) for i in range(n - share)])
    right = lax.ppermute(x[:, :EDGE], "tm", [(i + share, i) for i in range(n - share)])
    mine = spectra(x, left, right, share).reshape(2, n, bins, count)
    mine = lax.all_to_all(mine.transpose(1, 0, 2, 3), "tm", split_axis=0, concat_axis=0, tiled=True)
    mine = mine.reshape(SUBWIN, share, 2, bins, count).transpose(0, 2, 3, 1, 4)
    gathered = lax.all_gather(mine.reshape(rows, share * count), "pairs", axis=1, tiled=True)
    return correlate(gathered, station_order, block_list, bins)


def solution(mesh):
    placed = (P("pairs", "tm"), P(), P("pairs", None))
    return jax.shard_map(
        local, mesh=mesh, in_specs=placed, out_specs=P("pairs", "tm", None, None), check_vma=False
    )
```

time: 105 us -> 78.6 us (0.75)
  the two profiles are of different devices: /device:TPU:25 before, /device:TPU:0 now
where the time goes in v2:
time: 78.6 us; the launch traced here: 77 us
  Pallas kernels  76.3 us (97%)
    pallas_call x1, Pallas kernels, fused(): pl.pallas_call(functools.partial(fused_kernel, n, bins, blocks), grid=(bl...  61.4 us
    pallas_call x1, Pallas kernels, correlate(): pl.pallas_call(functools.partial(pairs_kernel, bins, step), grid_spec=plt...  14.9 us

profile of v2, /device:TPU:0, one launch (start us, length us, event | category | flops | bytes accessed | tf_op | source)
XLA Modules:
  0.0 77.0 jit_solution(2520815931026284273)
XLA Ops:
  0.0 0.8 copy.5.blocks_ref
  0.8 0.0 copy-start
  0.8 61.4 %shard_map.46 = bf16[16,48,2048]{2,1,0:T(8,128)(2,1)S(1)} custom-call(bf16[1024,4096]{1,0:T(8,128)(2,1)} %x_ref.1, bf16[1024,4096]{1,0:T(8,128)(2,1)} %x_ref.1, bf16[768,4096]{1,0:T(8,128)(2,1)} %constant.2.clone.table_hbm), custom_call_target="tpu_custom_call" | custom-call | tf_op jit(solution)/shard_map/pallas_call | solution.py:219
  62.2 0.0 copy-done
  62.2 14.9 %shard_map.47 = bf16[10,24,64,128]{3,2,1,0:T(8,128)(2,1)} custom-call(s32[10,2]{1,0:T(8,128)S(1)} %copy.5.blocks_ref, s32[16,128]{1,0:T(8,128)S(1)} %bitcast.8, bf16[768,2048]{1,0:T(8,128)(2,1)S(1)} %bitcast.7), custom_call_target="tpu_custom_call" | custom-call | tf_op jit(solution)/shard_map/pallas_call | solution.py:309
Async XLA Ops:
  0.8 61.4 %copy-start = (s32[2048]{0:T(1024)S(1)}, s32[2048]{0:T(1024)}, u32[]{:S(2)}) copy-start(s32[2048]{0:T(1024)} %param.5) | copy-start | bytes 24580

commit v3 on v2

--- a/solution.py
+++ b/solution.py
@@ -20,6 +20,8 @@
 EPS = 1e-06
 
 EDGE = 128
+NEAR = 8
+Z_SLOTS = 8
 TILE = 256
 MIB = 1 << 20
 MESH = pl.DeviceIdType.MESH
@@ -33,8 +35,8 @@
     return both.reshape(2 * BINS, SAMPLES).astype(np.float32).astype(jnp.bfloat16)
 
 
-def normalise(x_ref, norm_ref, mag_ref, band_ref, start):
-    for n in range(SAMPLES // TILE):
+def normalise(x_ref, norm_ref, mag_ref, band_ref, start, tiles):
+    for n in tiles:
         cols = slice(n * TILE, (n + 1) * TILE)
         sums = jnp.dot(
             mag_ref[:, n * TILE : (n + 1) * TILE + 2 * EDGE], band_ref[...], preferred_element_type=jnp.float32
@@ -73,7 +75,7 @@
     mag_ref[:, :EDGE] = jnp.abs(left_ref[...])
     mag_ref[:, EDGE : EDGE + SAMPLES] = jnp.abs(x_ref[...])
     mag_ref[:, EDGE + SAMPLES :] = jnp.abs(right_ref[...])
-    normalise(x_ref, norm_ref, mag_ref, band_ref, lax.div(lax.axis_index("tm"), share) * SAMPLES)
+    normalise(x_ref, norm_ref, mag_ref, band_ref, lax.div(lax.axis_index("tm"), share) * SAMPLES, range(SAMPLES // TILE))
     out_ref[...] = transform(table_ref, norm_ref, BINS)
 
 
@@ -102,6 +104,13 @@
     )(x, left, right, jnp.asarray(table_rows(BINS)))
 
 
+def partner(t, d):
+    for bit in (1, 2, 4, 8):
+        if d & bit:
+            t = t + bit * (1 - 2 * lax.rem(lax.div(t, bit), 2))
+    return t
+
+
 def fused_kernel(n, bins, blocks, rec_ref, x_ref, table_hbm, got_ref, mag_ref, norm_ref, band_ref, table_ref,
                  left_ref, right_ref, mine_ref, table_sem, edge_send, edge_recv, own_sem, send_sem, recv_sem,
                  hop_send, hop_recv):
@@ -113,12 +122,13 @@
     other = 1 - p
     after, before = lax.rem(t + 1, n), lax.rem(t + n - 1, n)
     table_copy = pltpu.make_async_copy(table_hbm, table_ref, table_sem)
+    partners = [partner(t, d) for d in range(n)]
 
     def columns(block):
         return pl.ds(pl.multiple_of(p * count + block * rows, 128), rows)
 
     def direct(block, d):
-        to = lax.rem(t + d, n)
+        to = partners[d]
         return pltpu.make_async_remote_copy(
             src_ref=mine_ref.at[block, to],
             dst_ref=got_ref.at[t, :, columns(block)],
@@ -128,10 +138,21 @@
             device_id_type=MESH,
         )
 
+    def across(block, d):
+        to = partners[d]
+        return pltpu.make_async_remote_copy(
+            src_ref=mine_ref.at[block, to],
+            dst_ref=got_ref.at[t, :, columns(block)],
+            send_sem=hop_send.at[block, d],
+            recv_sem=hop_recv.at[block, d],
+            device_id=(to, other),
+            device_id_type=MESH,
+        )
+
     def hop(block, d):
-        source = lax.rem(t + n - d, n)
+        source = partners[d]
         return pltpu.make_async_remote_copy(
-            src_ref=got_ref.at[source, :, columns(block)] if d else mine_ref.at[block, t],
+            src_ref=got_ref.at[source, :, columns(block)],
             dst_ref=got_ref.at[source, :, columns(block)],
             send_sem=hop_send.at[block, d],
             recv_sem=hop_recv.at[block, d],
@@ -143,20 +164,12 @@
         return pltpu.make_async_copy(mine_ref.at[block, t], got_ref.at[t, :, columns(block)], own_sem.at[block])
 
     def forward(block):
-        for d in range(1, n):
+        for d in range(NEAR, n):
             direct(block, d).wait_recv()
             hop(block, d).start()
 
-    @pl.when(i == 0)
-    def _():
-        table_copy.start()
-        barrier = pltpu.get_barrier_semaphore()
-        for d in range(1, n):
-            pl.semaphore_signal(barrier, inc=1, device_id=(lax.rem(t + d, n), p), device_id_type=MESH)
-        pl.semaphore_signal(barrier, inc=1, device_id=(t, other), device_id_type=MESH)
-        fill_band(band_ref)
-        pl.semaphore_wait(barrier, n)
-        edges = [
+    def edges():
+        return [
             pltpu.make_async_remote_copy(
                 src_ref=rec_ref.at[:, pl.ds(first, EDGE)],
                 dst_ref=landing,
@@ -169,27 +182,46 @@
                 [(SAMPLES - EDGE, left_ref, after), (0, right_ref, before)]
             )
         ]
-        for edge in edges:
+
+    @pl.when(i == 0)
+    def _():
+        table_copy.start()
+        barrier = pltpu.get_barrier_semaphore()
+        for d in range(1, n):
+            pl.semaphore_signal(barrier, inc=1, device_id=(partners[d], p), device_id_type=MESH)
+        for d in range(NEAR):
+            pl.semaphore_signal(barrier, inc=1, device_id=(partners[d], other), device_id_type=MESH)
+        fill_band(band_ref)
+        pl.semaphore_wait(barrier, n - 1 + NEAR)
+        for edge in edges():
             edge.start()
-        for edge in edges:
+
+    mag_ref[:, EDGE : EDGE + SAMPLES] = jnp.abs(x_ref[...])
+    last = SAMPLES // TILE - 1
+    normalise(x_ref, norm_ref, mag_ref, band_ref, t * SAMPLES, range(1, last))
+
+    @pl.when(i == 0)
+    def _():
+        for edge in edges():
             edge.wait()
 
     at = pl.ds(pl.multiple_of(i * rows, rows), rows)
     left = jnp.abs(left_ref[at, :])
     right = jnp.abs(right_ref[at, :])
     mag_ref[:, :EDGE] = jnp.where(t == 0, jnp.zeros_like(left), left)
-    mag_ref[:, EDGE : EDGE + SAMPLES] = jnp.abs(x_ref[...])
     mag_ref[:, EDGE + SAMPLES :] = jnp.where(t == n - 1, jnp.zeros_like(right), right)
-    normalise(x_ref, norm_ref, mag_ref, band_ref, t * SAMPLES)
+    normalise(x_ref, norm_ref, mag_ref, band_ref, t * SAMPLES, (0, last))
 
     @pl.when(i == 0)
     def _():
         table_copy.wait()
 
     mine_ref[i] = transform(table_ref, norm_ref, bins)
-    for d in range(1, n):
+    for d in range(n - 1, 0, -1):
         direct(i, d).start()
-    hop(i, 0).start()
+        if d < NEAR:
+            across(i, d).start()
+    across(i, 0).start()
     own(i).start()
 
     @pl.when(i > 0)
@@ -203,9 +235,13 @@
         def finish(block, carry):
             own(block).wait()
             for d in range(n):
-                if d:
+                if d >= NEAR:
                     direct(block, d).wait_send()
-                hop(block, d).wait()
+                    hop(block, d).wait()
+                else:
+                    if d:
+                        direct(block, d).wait()
+                    across(block, d).wait()
             return carry
 
         lax.fori_loop(0, blocks, finish, 0)
@@ -265,40 +301,46 @@
     return jnp.where(live, ids, -1)
 
 
-def pairs_kernel(bins, step, blocks_ref, order_ref, x_ref, out_ref, y_ref):
+def pairs_kernel(bins, step, blocks_ref, order_ref, x_ref, out_ref, y_ref, z_ref):
     ids = []
     lane = lax.broadcasted_iota(jnp.int32, (1, 128), 1)
-    left_lanes = lane % GSIZE // 2 * 2 + lane // GSIZE
+    left_lanes = lane % (GSIZE // 2) * 2 + lane % GSIZE // (GSIZE // 2)
     right_lanes = lane % GSIZE
     for s in range(step):
         k = pl.program_id(0) * step + s
         live = blocks_ref[k, 0] >= 0
-        ids.append(slot_ids(order_ref, blocks_ref[k, 0], live, left_lanes))
-        ids.append(slot_ids(order_ref, blocks_ref[k, 1], live, right_lanes))
+        left = slot_ids(order_ref, blocks_ref[k, 0], live, left_lanes)
+        right = slot_ids(order_ref, blocks_ref[k, 1], live, right_lanes)
+        ids.append(jnp.where(lane < GSIZE, left, right))
     wanted = jnp.concatenate(ids, axis=1)
-    station = lax.broadcasted_iota(jnp.int32, (x_ref.shape[1], step * 256), 0)
+    station = lax.broadcasted_iota(jnp.int32, (x_ref.shape[1], step * 128), 0)
     pick = jnp.where(station == wanted, 1.0, 0.0).astype(jnp.bfloat16)
     total = jnp.dot(x_ref[...], pick, preferred_element_type=jnp.float32)
-    for n in range(2 * step):
+    for n in range(step):
         y_ref[n] = total[:, n * 128 : (n + 1) * 128]
-    lane = lax.broadcasted_iota(jnp.int32, (SUBWIN, 128), 1)
-    straight = lane % 2 == 0
-    low = lax.broadcasted_iota(jnp.int32, (GSIZE, 128), 1) < GSIZE
+    half = GSIZE // 2
+    low = lax.broadcasted_iota(jnp.int32, (SUBWIN, 128), 1) < GSIZE
+    low_out = lax.broadcasted_iota(jnp.int32, (half, 128), 1) < GSIZE
     for f in range(bins):
         for s in range(step):
-            re_a = y_ref[2 * s, pl.ds(f, SUBWIN, stride=2 * bins), :]
-            im_a = y_ref[2 * s, pl.ds(bins + f, SUBWIN, stride=2 * bins), :]
-            re_b = y_ref[2 * s + 1, pl.ds(f, SUBWIN, stride=2 * bins), :]
-            im_b = y_ref[2 * s + 1, pl.ds(bins + f, SUBWIN, stride=2 * bins), :]
-            a_rows = jnp.concatenate(
-                [jnp.where(straight, re_a, -im_a), jnp.where(straight, im_a, re_a)], axis=0
-            ).astype(jnp.bfloat16)
-            b_rows = jnp.concatenate([re_b, im_b], axis=0).astype(jnp.bfloat16)
+            re = y_ref[s, pl.ds(f, SUBWIN, stride=2 * bins), :]
+            im = y_ref[s, pl.ds(bins + f, SUBWIN, stride=2 * bins), :]
+            re_swap = pltpu.roll(re, GSIZE, 1)
+            im_swap = pltpu.roll(im, GSIZE, 1)
+            a_rows = jnp.concatenate([jnp.where(low, re, -im_swap), jnp.where(low, im, re_swap)], axis=0)
+            b_rows = jnp.concatenate([jnp.where(low, re_swap, re), jnp.where(low, im_swap, im)], axis=0)
             full = lax.dot_general(
-                a_rows, b_rows, (((0,), (0,)), ((), ())), preferred_element_type=jnp.float32
-            )
-            kept = jnp.where(low, full[:GSIZE], full[GSIZE:]) * (1.0 / SUBWIN)
-            out_ref[s, f] = kept.astype(jnp.bfloat16)
+                a_rows.astype(jnp.bfloat16),
+                b_rows.astype(jnp.bfloat16),
+                (((0,), (0,)), ((), ())),
+                preferred_element_type=jnp.float32,
+            ) * (1.0 / SUBWIN)
+            slot = (f * step + s) % Z_SLOTS
+            for c in range(2):
+                base = c * GSIZE
+                kept = jnp.where(low_out, full[base : base + half], full[base + half : base + GSIZE])
+                z_ref[slot, pl.ds(c, half, stride=2), :] = kept
+            out_ref[s, f] = z_ref[slot].astype(jnp.bfloat16)
 
 
 def correlate(x, station_order, block_list, bins):
@@ -316,7 +358,10 @@
                 pl.BlockSpec((rows, stations), lambda i, b: (0, 0)),
             ],
             out_specs=pl.BlockSpec((step, bins, GSIZE, 128), lambda i, b: (i, 0, 0, 0)),
-            scratch_shapes=[pltpu.VMEM((2 * step, rows, 128), jnp.float32)],
+            scratch_shapes=[
+                pltpu.VMEM((step, rows, 128), jnp.float32),
+                pltpu.VMEM((Z_SLOTS, GSIZE, 128), jnp.float32),
+            ],
         ),
         out_shape=jax.ShapeDtypeStruct((slots, bins, GSIZE, 128), jnp.bfloat16),
         compiler_params=pltpu.CompilerParams(vmem_limit_bytes=48 * MIB),

time: 78.6 us -> 77.4 us (0.985); the launches traced: 77 us -> 77.2 us
    pallas_call x1, Pallas kernels: 14.9 us -> 16.2 us  [correlate(): pl.pallas_call(functools.partial(pairs_kernel, bins, step), grid_spec=plt...]
    pallas_call x1, Pallas kernels: 61.4 us -> 60.2 us  [fused(): pl.pallas_call(functools.partial(fused_kernel, n, bins, blocks), grid=(bl...]
where the time goes in v3:
time: 77.4 us; the launch traced here: 77.2 us
  Pallas kernels  76.5 us (99%)
    pallas_call x1, Pallas kernels, fused(): pl.pallas_call(functools.partial(fused_kernel, n, bins, blocks), grid=(bl...  60.2 us
    pallas_call x1, Pallas kernels, correlate(): pl.pallas_call(functools.partial(pairs_kernel, bins, step), grid_spec=plt...  16.2 us

profile of v3, /device:TPU:0, one launch (start us, length us, event | category | flops | bytes accessed | tf_op | source)
XLA Modules:
  0.0 77.2 jit_solution(13255482860083894872)
XLA Ops:
  0.0 0.8 copy.5.blocks_ref
  0.8 0.0 copy-start
  0.8 60.2 %shard_map.46 = bf16[16,48,2048]{2,1,0:T(8,128)(2,1)S(1)} custom-call(bf16[1024,4096]{1,0:T(8,128)(2,1)} %x_ref.1, bf16[1024,4096]{1,0:T(8,128)(2,1)} %x_ref.1, bf16[768,4096]{1,0:T(8,128)(2,1)} %constant.2.clone.table_hbm), custom_call_target="tpu_custom_call" | custom-call | tf_op jit(solution)/shard_map/pallas_call | solution.py:255
  61.0 0.0 copy-done
  61.0 16.2 %shard_map.47 = bf16[10,24,64,128]{3,2,1,0:T(8,128)(2,1)} custom-call(s32[10,2]{1,0:T(8,128)S(1)} %copy.5.blocks_ref, s32[16,128]{1,0:T(8,128)S(1)} %bitcast.8, bf16[768,2048]{1,0:T(8,128)(2,1)S(1)} %bitcast.7), custom_call_target="tpu_custom_call" | custom-call | tf_op jit(solution)/shard_map/pallas_call | solution.py:351
Async XLA Ops:
  0.8 60.2 %copy-start = (s32[2048]{0:T(1024)S(1)}, s32[2048]{0:T(1024)}, u32[]{:S(2)}) copy-start(s32[2048]{0:T(1024)} %param.5) | copy-start | bytes 24580

commit v4 on v3

--- a/solution.py
+++ b/solution.py
@@ -21,7 +21,6 @@
 
 EDGE = 128
 NEAR = 8
-Z_SLOTS = 8
 TILE = 256
 MIB = 1 << 20
 MESH = pl.DeviceIdType.MESH
@@ -224,12 +223,13 @@
     across(i, 0).start()
     own(i).start()
 
-    @pl.when(i > 0)
-    def _():
-        forward(i - 1)
+    @pl.when(i > 1)
+    def _():
+        forward(i - 2)
 
     @pl.when(i == blocks - 1)
     def _():
+        forward(blocks - 2)
         forward(blocks - 1)
 
         def finish(block, carry):
@@ -301,46 +301,40 @@
     return jnp.where(live, ids, -1)
 
 
-def pairs_kernel(bins, step, blocks_ref, order_ref, x_ref, out_ref, y_ref, z_ref):
+def pairs_kernel(bins, step, blocks_ref, order_ref, x_ref, out_ref, y_ref):
     ids = []
     lane = lax.broadcasted_iota(jnp.int32, (1, 128), 1)
-    left_lanes = lane % (GSIZE // 2) * 2 + lane % GSIZE // (GSIZE // 2)
+    left_lanes = lane % GSIZE // 2 * 2 + lane // GSIZE
     right_lanes = lane % GSIZE
     for s in range(step):
         k = pl.program_id(0) * step + s
         live = blocks_ref[k, 0] >= 0
-        left = slot_ids(order_ref, blocks_ref[k, 0], live, left_lanes)
-        right = slot_ids(order_ref, blocks_ref[k, 1], live, right_lanes)
-        ids.append(jnp.where(lane < GSIZE, left, right))
+        ids.append(slot_ids(order_ref, blocks_ref[k, 0], live, left_lanes))
+        ids.append(slot_ids(order_ref, blocks_ref[k, 1], live, right_lanes))
     wanted = jnp.concatenate(ids, axis=1)
-    station = lax.broadcasted_iota(jnp.int32, (x_ref.shape[1], step * 128), 0)
+    station = lax.broadcasted_iota(jnp.int32, (x_ref.shape[1], step * 256), 0)
     pick = jnp.where(station == wanted, 1.0, 0.0).astype(jnp.bfloat16)
     total = jnp.dot(x_ref[...], pick, preferred_element_type=jnp.float32)
-    for n in range(step):
+    for n in range(2 * step):
         y_ref[n] = total[:, n * 128 : (n + 1) * 128]
-    half = GSIZE // 2
-    low = lax.broadcasted_iota(jnp.int32, (SUBWIN, 128), 1) < GSIZE
-    low_out = lax.broadcasted_iota(jnp.int32, (half, 128), 1) < GSIZE
+    lane = lax.broadcasted_iota(jnp.int32, (SUBWIN, 128), 1)
+    straight = lane % 2 == 0
+    low = lax.broadcasted_iota(jnp.int32, (GSIZE, 128), 1) < GSIZE
     for f in range(bins):
         for s in range(step):
-            re = y_ref[s, pl.ds(f, SUBWIN, stride=2 * bins), :]
-            im = y_ref[s, pl.ds(bins + f, SUBWIN, stride=2 * bins), :]
-            re_swap = pltpu.roll(re, GSIZE, 1)
-            im_swap = pltpu.roll(im, GSIZE, 1)
-            a_rows = jnp.concatenate([jnp.where(low, re, -im_swap), jnp.where(low, im, re_swap)], axis=0)
-            b_rows = jnp.concatenate([jnp.where(low, re_swap, re), jnp.where(low, im_swap, im)], axis=0)
+            re_a = y_ref[2 * s, pl.ds(f, SUBWIN, stride=2 * bins), :]
+            im_a = y_ref[2 * s, pl.ds(bins + f, SUBWIN, stride=2 * bins), :]
+            re_b = y_ref[2 * s + 1, pl.ds(f, SUBWIN, stride=2 * bins), :]
+            im_b = y_ref[2 * s + 1, pl.ds(bins + f, SUBWIN, stride=2 * bins), :]
+            a_rows = jnp.concatenate(
+                [jnp.where(straight, re_a, -im_a), jnp.where(straight, im_a, re_a)], axis=0
+            ).astype(jnp.bfloat16)
+            b_rows = jnp.concatenate([re_b, im_b], axis=0).astype(jnp.bfloat16)
             full = lax.dot_general(
-                a_rows.astype(jnp.bfloat16),
-                b_rows.astype(jnp.bfloat16),
-                (((0,), (0,)), ((), ())),
-                preferred_element_type=jnp.float32,
-            ) * (1.0 / SUBWIN)
-            slot = (f * step + s) % Z_SLOTS
-            for c in range(2):
-                base = c * GSIZE
-                kept = jnp.where(low_out, full[base : base + half], full[base + half : base + GSIZE])
-                z_ref[slot, pl.ds(c, half, stride=2), :] = kept
-            out_ref[s, f] = z_ref[slot].astype(jnp.bfloat16)
+                a_rows, b_rows, (((0,), (0,)), ((), ())), preferred_element_type=jnp.float32
+            )
+            kept = jnp.where(low, full[:GSIZE], full[GSIZE:]) * (1.0 / SUBWIN)
+            out_ref[s, f] = kept.astype(jnp.bfloat16)
 
 
 def correlate(x, station_order, block_list, bins):
@@ -358,10 +352,7 @@
                 pl.BlockSpec((rows, stations), lambda i, b: (0, 0)),
             ],
             out_specs=pl.BlockSpec((step, bins, GSIZE, 128), lambda i, b: (i, 0, 0, 0)),
-            scratch_shapes=[
-                pltpu.VMEM((step, rows, 128), jnp.float32),
-                pltpu.VMEM((Z_SLOTS, GSIZE, 128), jnp.float32),
-            ],
+            scratch_shapes=[pltpu.VMEM((2 * step, rows, 128), jnp.float32)],
         ),
         out_shape=jax.ShapeDtypeStruct((slots, bins, GSIZE, 128), jnp.bfloat16),
         compiler_params=pltpu.CompilerParams(vmem_limit_bytes=48 * MIB),

time: 77.4 us -> 76 us (0.982)
  Pallas kernels: 76.5 us -> 75.1 us
    pallas_call x1, Pallas kernels: 16.2 us -> 14.9 us  [correlate(): pl.pallas_call(functools.partial(pairs_kernel, bins, step), grid_spec=plt...]
where the time goes in v4:
time: 76 us; the launch traced here: 75.9 us
  Pallas kernels  75.1 us (99%)
  local copies, waits for them, and re-layouts  0.77 us (1%)
    pallas_call x1, Pallas kernels, fused(): pl.pallas_call(functools.partial(fused_kernel, n, bins, blocks), grid=(bl...  60.2 us
    pallas_call x1, Pallas kernels, correlate(): pl.pallas_call(functools.partial(pairs_kernel, bins, step), grid_spec=plt...  14.9 us

profile of v4, /device:TPU:0, one launch (start us, length us, event | category | flops | bytes accessed | tf_op | source)
XLA Modules:
  0.0 75.9 jit_solution(9045108469182880190)
XLA Ops:
  0.0 0.8 %copy.5.blocks_ref = s32[10,2]{1,0:T(8,128)S(1)} copy(s32[10,2]{0,1:T(2,128)} %param.6) | data formatting | bytes 160 | tf_op args[2]
  0.8 0.0 copy-start
  0.8 60.2 %shard_map.46 = bf16[16,48,2048]{2,1,0:T(8,128)(2,1)S(1)} custom-call(bf16[1024,4096]{1,0:T(8,128)(2,1)} %x_ref.1, bf16[1024,4096]{1,0:T(8,128)(2,1)} %x_ref.1, bf16[768,4096]{1,0:T(8,128)(2,1)} %constant.2.clone.table_hbm), custom_call_target="tpu_custom_call" | custom-call | tf_op jit(solution)/shard_map/pallas_call | solution.py:255
  61.0 0.0 copy-done
  61.0 14.9 %shard_map.47 = bf16[10,24,64,128]{3,2,1,0:T(8,128)(2,1)} custom-call(s32[10,2]{1,0:T(8,128)S(1)} %copy.5.blocks_ref, s32[16,128]{1,0:T(8,128)S(1)} %bitcast.8, bf16[768,2048]{1,0:T(8,128)(2,1)S(1)} %bitcast.7), custom_call_target="tpu_custom_call" | custom-call | tf_op jit(solution)/shard_map/pallas_call | solution.py:345
Async XLA Ops:
  0.8 60.2 %copy-start = (s32[2048]{0:T(1024)S(1)}, s32[2048]{0:T(1024)}, u32[]{:S(2)}) copy-start(s32[2048]{0:T(1024)} %param.5) | copy-start | bytes 24580
